TPU v7x, 32 devices: a whole 2x2x4 slice. The times are simulated.
32 devices in a mesh: grp: 2 (over x), ch: 4 (over y, core), sp: 4 (over z).
Axes of the slice: x: 2, y: 2, z: 4, core: 2. Of those that a mesh axis runs over, the one named last changes fastest.
Arguments:
- features: bfloat16 [1024, 64, 128], P(('grp', 'ch'), 'sp'), parts along dimension 0, may hold values from -6 to 6
- saved_mix: bfloat16 [1024, 64, 128], P(('grp', 'ch'), 'sp'), parts along dimension 0, may hold values from -6 to 6
- out_grad: bfloat16 [1024, 64, 128], P(('grp', 'ch'), 'sp'), parts along dimension 0, may hold values from -6 to 6
- kernel: bfloat16 [512, 31, 31], P('ch'), may hold values from -0.1875 to 0.1875
- w_in: bfloat16 [512, 2048], P(None, 'ch'), may hold values from -0.25 to 0.25
- w_out: bfloat16 [2048, 512], P('ch'), may hold values from -0.125 to 0.125
Outputs:
- in_grad: float32 [1024, 64, 128], P(('grp', 'ch'), 'sp'), parts along dimension 0
- kernel_grad: float32 [1024, 31, 31], P(('grp', 'ch')), parts along dimension 0
- w_in_grad: float32 [1024, 2048], P('grp', ('ch', 'sp')), parts along dimension 0
- w_out_grad: float32 [4096, 512], P(('grp', 'ch', 'sp')), parts along dimension 0
There are 2 independent parts, one for each index of `grp`. A program takes and returns all parts, laid end to end along the dimension named above; an argument that names none is the same for every part. Nothing has to cross between parts.
All inputs are finite; a program needn't handle non-finite values.
Results may differ from a plain program's by a relative error of at most 0.0041.
Values may be sent and summed in bfloat16 or wider, within the bound.
A program may use at most 64 MiB of HBM per device.

v0:
```python
import math
import jax
import jax.numpy as jnp
from jax import lax
from jax.sharding import PartitionSpec as P

SQRT_HALF = 0.7071067811865476
INV_ROOT_TAU = 0.3989422804014327


def with_halo(block, sides, width):
    for axis, dim in sides:
        count = lax.axis_size(axis)
        forward = [(i, i + 1) for i in range(count - 1)]
        backward = [(target, source) for source, target in forward]
        low = lax.ppermute(
            lax.slice_in_dim(block, block.shape[dim] - width, None, axis=dim), axis, forward
        )
        high = lax.ppermute(lax.slice_in_dim(block, 0, width, axis=dim), axis, backward)
        block = jnp.concatenate([low, block, high], axis=dim)
    return block


def depthwise(source, taps):
    return lax.conv_general_dilated(
        source[None],
        taps[:, None],
        (1, 1),
        "VALID",
        dimension_numbers=("NCHW", "OIHW", "NCHW"),
        feature_group_count=source.shape[0],
        preferred_element_type=jnp.float32,
    )[0]


def contract_last(left, right):
    return lax.dot_general(
        left, right, (((1,), (1,)), ((), ())), preferred_element_type=jnp.float32
    )


def contract_first(left, right):
    return lax.dot_general(
        left, right, (((0,), (0,)), ((), ())), preferred_element_type=jnp.float32
    )


def pointwise_back(mixed_rows, grad_rows, w_in_block, w_out_block):
    preact = contract_first(w_in_block, mixed_rows)
    normal_cdf = 0.5 * (1.0 + jax.scipy.special.erf(preact * SQRT_HALF))
    normal_pdf = INV_ROOT_TAU * jnp.exp(-0.5 * preact * preact)
    hidden = (preact * normal_cdf).astype(jnp.bfloat16)
    hidden_grad = jnp.dot(w_out_block, grad_rows, preferred_element_type=jnp.float32)
    preact_grad = (hidden_grad * (normal_cdf + preact * normal_pdf)).astype(jnp.bfloat16)
    return (hidden, preact_grad)


def per_device(features, saved_mix, out_grad, kernel, w_in, w_out):
    local_ch, rows, width = features.shape
    local_pos = rows * width
    half = kernel.shape[1] // 2
    factor = 1.0 / math.sqrt(local_pos * lax.axis_size("sp"))
    mixed_rows = saved_mix.reshape(local_ch, local_pos)
    grad_rows = out_grad.reshape(local_ch, local_pos)
    mixed_all, grad_all = (
        lax.all_gather(mixed_rows, "ch", axis=0, tiled=True),
        lax.all_gather(grad_rows, "ch", axis=0, tiled=True),
    )
    hidden, preact_grad = pointwise_back(mixed_all, grad_all, w_in, w_out)
    w_in_local = contract_last(mixed_all, preact_grad)
    w_out_local = contract_last(grad_all, hidden)
    mix_grad = lax.psum_scatter(
        jnp.dot(w_in, preact_grad, preferred_element_type=jnp.float32),
        "ch",
        scatter_dimension=0,
        tiled=True,
    ).astype(jnp.bfloat16)
    w_in_sum, w_out_sum = (
        lax.psum_scatter(w_in_local, "sp", scatter_dimension=1, tiled=True),
        lax.psum_scatter(w_out_local, "sp", scatter_dimension=1, tiled=True),
    )
    mix_grad = mix_grad.reshape(local_ch, rows, width)
    rimmed = with_halo(mix_grad, (("sp", 1),), half)
    padded = jnp.pad(rimmed, ((0, 0), (0, 0), (half, half)))
    in_grad = out_grad.astype(jnp.float32) + depthwise(padded, kernel[:, ::-1, ::-1])
    kernel_part = depthwise(padded, features)
    kernel_grad = lax.psum(kernel_part, "sp")[:, ::-1, ::-1] * factor
    return (in_grad, kernel_grad, w_in_sum * factor, w_out_sum.T * factor)


def solution(mesh):
    return jax.shard_map(
        per_device,
        mesh=mesh,
        in_specs=(
            P(("grp", "ch"), "sp", None),
            P(("grp", "ch"), "sp", None),
            P(("grp", "ch"), "sp", None),
            P("ch", None, None),
            P(None, "ch"),
            P("ch", None),
        ),
        out_specs=(
            P(("grp", "ch"), "sp", None),
            P(("grp", "ch"), None, None),
            P("grp", ("ch", "sp")),
            P(("grp", "ch", "sp"), None),
        ),
        check_vma=False,
    )
```

profile of v0, /device:TPU:0, one launch (start us, length us, event | category | flops | bytes accessed | tf_op | source)
XLA Modules:
  0.0 533.9 jit_solution(92826388484412066)
XLA Ops:
  7.2 0.0 copy-start
  7.2 0.0 all-gather.5.cloned.1.call-start
  7.2 2.0 copy.34
  9.2 0.0 all-gather.5.cloned.1.call-update
  9.3 0.0 all-gather.3.cloned.1.call-start
  9.3 2.0 copy.35
  11.3 0.0 copy-start.7
  11.3 0.0 all-gather.3.cloned.1.call-update
  11.3 0.0 reduce-scatter.4.cloned.1.call-start
  11.4 24.1 %all-gather.5.cloned.1.call-done = bf16[512,2048]{1,0:T(8,128)(2,1)} async-done(((bf16[128,2048]{1,0:T(8,128)(2,1)}), bf16[512,2048]{1,0:T(8,128)(2,1)}) %all-gather.5.cloned.1.call-update) | async-done | bytes 2097168 | tf_op jit(solution)/shard_map/all_gather | solution.py:66
  35.5 0.0 copy-done
  35.5 4.8 fusion.21
  40.3 19.3 %all-gather.3.cloned.1.call-done = bf16[512,2048]{1,0:T(8,128)(2,1)} async-done(((bf16[128,2048]{1,0:T(8,128)(2,1)}), bf16[512,2048]{1,0:T(8,128)(2,1)}) %all-gather.3.cloned.1.call-update) | async-done | bytes 2097168 | tf_op jit(solution)/shard_map/all_gather | solution.py:67
  59.7 0.0 copy-done.7
  59.7 4.6 fusion.5
  64.3 3.3 convolution_bitcast_fusion
  67.6 0.0 reduce-scatter.4.cloned.1.call-update
  67.6 0.0 reduce-scatter.6.cloned.1.call-start
  67.6 3.9 convolution_bitcast_fusion.1
  71.5 0.0 reduce-scatter.6.cloned.1.call-update
  71.6 0.0 reduce-scatter.8.cloned.1.call-start
  71.6 5.8 %fusion.18 = f32[512,512]{0,1:T(8,128)} fusion(bf16[512,2048]{1,0:T(8,128)(2,1)} %all-gather.3.cloned.1.call-done, f32[512,2048]{1,0:T(8,128)} %fusion.21), kind=kOutput, calls=%fused_computation.24 | convolution fusion | flops 1078984704 | bytes 7340032 | tf_op jit(solution)/shard_map/dot_general | solution.py:37
  77.4 0.0 copy-start.2
  77.4 0.0 copy-start.6
  77.4 0.0 copy-start.4
  77.4 0.0 reduce-scatter.8.cloned.1.call-update
  77.5 0.0 all-reduce.3.cloned.1.call-start
  77.5 34.7 %reduce-scatter.4.cloned.1.call-done = f32[128,2048]{0,1:T(8,128)} async-done(((f32[512,2048]{0,1:T(8,128)}), f32[128,2048]{0,1:T(8,128)}) %reduce-scatter.4.cloned.1.call-update) | async-done | bytes 1048592 | tf_op jit(solution)/shard_map/reduce_scatter | solution.py:72
  112.2 1.3 convert_element_type.16
  113.5 1.0 fusion.20
  114.5 3.4 collective-permute-start
  117.9 1.5 collective-permute-start.1
  119.4 0.0 copy-done.2
  119.4 1.2 copy.15
  120.7 0.0 copy-done.6
  120.7 0.9 rev.6
  121.5 0.0 copy-done.4
  121.5 1.5 copy.19
  123.0 28.5 %reduce-scatter.6.cloned.1.call-done = f32[512,128]{0,1:T(8,128)} async-done(((f32[512,512]{0,1:T(8,128)}), f32[512,128]{0,1:T(8,128)}) %reduce-scatter.6.cloned.1.call-update) | async-done | bytes 262160 | tf_op jit(solution)/shard_map/reduce_scatter | solution.py:79
  151.5 1.0 broadcast_multiply_fusion.1
  152.5 0.8 copy.21
  153.3 25.4 %reduce-scatter.8.cloned.1.call-done = f32[512,128]{0,1:T(8,128)} async-done(((f32[512,512]{0,1:T(8,128)}), f32[512,128]{0,1:T(8,128)}) %reduce-scatter.8.cloned.1.call-update) | async-done | bytes 262160 | tf_op jit(solution)/shard_map/reduce_scatter | solution.py:80
  178.7 0.0 copy-start.3
  178.7 1.8 multiply_bitcast_fusion
  180.4 0.0 collective-permute-done
  180.4 0.0 copy-start.5
  180.4 0.8 copy-done.5
  181.2 0.0 collective-permute-done.1
  181.2 1.8 fusion.17
  183.0 0.0 copy-done.3
  183.0 173.5 %fusion.7 = f32[1,128,31,31]{1,0,3,2:T(1,128)S(1)} fusion(bf16[128,1,16,128]{0,1,3,2:T(2,128)(2,1)S(1)} %copy-done.3, bf16[1,128,46,158]{1,3,2,0:T(8,128)(2,1)S(1)} %fusion.17), kind=kOutput, calls=%fused_computation.13 | convolution fusion | flops 503840768 | bytes 2876928 | tf_op jit(solution)/shard_map/conv_general_dilated | solution.py:25
  356.5 0.1 copy.36
  356.6 0.9 rev.7
  357.5 0.0 all-reduce.3.cloned.1.call-update
  357.5 0.0 copy-start.1
  357.6 166.1 %fusion.9 = f32[1,128,16,128]{1,0,3,2:T(1,128)S(1)} fusion(bf16[1,128,46,158]{1,3,2,0:T(8,128)(2,1)S(1)} %fusion.17, bf16[128,1,31,31]{0,3,2,1:T(8,128)(2,1)} %bitcast.44), kind=kOutput, calls=%fused_computation.15 | convolution fusion | flops 503840768 | bytes 3155200 | tf_op jit(solution)/shard_map/conv_general_dilated | solution.py:25
  523.7 0.0 copy-done.1
  523.7 0.1 convert_add_fusion
  523.8 1.4 copy.20
  525.2 0.0 all-reduce.3.cloned.1.call-done
  525.2 1.9 broadcast_multiply_fusion
Async XLA Ops:
  7.2 28.3 %copy-start = (bf16[512,512]{1,0:T(8,128)(2,1)S(1)}, bf16[512,512]{1,0:T(8,128)(2,1)}, u32[]{:S(2)}) copy-start(bf16[512,512]{1,0:T(8,128)(2,1)} %param.10) | copy-start | bytes 1572868
  7.2 28.3 %all-gather.5.cloned.1.call-start = ((), (), s32[]{:S(2)}) async-start(), calls=%async_computation.4 | async-start | bytes 2621440 | tf_op jit(solution)/shard_map/all_gather | solution.py:66
  9.3 50.4 %all-gather.3.cloned.1.call-start = ((), (), s32[]{:S(2)}) async-start(), calls=%async_computation.3 | async-start | bytes 2621440 | tf_op jit(solution)/shard_map/all_gather | solution.py:67
  11.3 48.4 %copy-start.7 = (bf16[512,512]{1,0:T(8,128)(2,1)S(1)}, bf16[512,512]{1,0:T(8,128)(2,1)}, u32[]{:S(2)}) copy-start(bf16[512,512]{1,0:T(8,128)(2,1)} %param.11) | copy-start | bytes 1572868
  11.3 100.9 %reduce-scatter.4.cloned.1.call-start = ((), (), s32[]{:S(2)}) async-start(), calls=%async_computation.5 | async-start | bytes 5242880 | tf_op jit(solution)/shard_map/reduce_scatter | solution.py:72
  67.6 83.9 %reduce-scatter.6.cloned.1.call-start = ((), (), s32[]{:S(2)}) async-start(), calls=%async_computation.7 | async-start | bytes 1310720 | tf_op jit(solution)/shard_map/reduce_scatter | solution.py:79
  71.6 107.1 %reduce-scatter.8.cloned.1.call-start = ((), (), s32[]{:S(2)}) async-start(), calls=%async_computation.8 | async-start | bytes 1310720 | tf_op jit(solution)/shard_map/reduce_scatter | solution.py:80
  77.4 42.0 %copy-start.2 = (bf16[128,16,128]{2,1,0:T(8,128)(2,1)S(1)}, bf16[128,16,128]{2,1,0:T(8,128)(2,1)}, u32[]{:S(2)}) copy-start(bf16[128,16,128]{2,1,0:T(8,128)(2,1)} %param.8) | copy-start | bytes 1572868
  77.4 43.2 %copy-start.6 = (bf16[128,31,31]{0,2,1:T(8,128)(2,1)S(1)}, bf16[128,31,31]{0,2,1:T(8,128)(2,1)}, u32[]{:S(2)}) copy-start(bf16[128,31,31]{0,2,1:T(8,128)(2,1)} %param.9) | copy-start | bytes 738052
  77.4 44.1 %copy-start.4 = (bf16[128,16,128]{2,1,0:T(8,128)(2,1)S(1)}, bf16[128,16,128]{2,1,0:T(8,128)(2,1)}, u32[]{:S(2)}) copy-start(bf16[128,16,128]{2,1,0:T(8,128)(2,1)} %param.6) | copy-start | bytes 1572868
  77.5 447.7 %all-reduce.3.cloned.1.call-start = ((), (), s32[]{:S(2)}) async-start(), calls=%async_computation.6 | async-start | bytes 1015808 | tf_op jit(solution)/shard_map/psum | solution.py:87
  114.5 65.9 %collective-permute-start = (bf16[128,15,128]{0,2,1:T(8,128)(2,1)}, bf16[128,15,128]{0,2,1:T(8,128)(2,1)S(1)}, u32[]{:S(2)}, u32[]{:S(2)}) collective-permute-start(bf16[128,15,128]{0,2,1:T(8,128)(2,1)} %get-tuple-element.12), channel_id=1, source_target_pairs={{0,1},{1,2},{2,3},{4,5},{5,6},{6,7},{8,9},{9,10},{10,11},{12,13},{... | collective-permute-start | bytes 1474568 | tf_op jit(solution)/shard_map/ppermute | solution.py:16
  117.9 63.3 %collective-permute-start.1 = (bf16[128,15,128]{0,2,1:T(8,128)(2,1)S(1)}, bf16[128,15,128]{0,2,1:T(8,128)(2,1)}, u32[]{:S(2)}, u32[]{:S(2)}) collective-permute-start(bf16[128,15,128]{0,2,1:T(8,128)(2,1)S(1)} %get-tuple-element.13), channel_id=1, source_target_pairs={{1,0},{2,1},{3,2},{5,4},{6,5},{7,6},{9,8},{10,9},{11,10},{13,12},{... | collective-permute-start | bytes 1474568 | tf_op jit(solution)/shard_map/ppermute | solution.py:19
  178.7 4.3 copy-start.3
  180.4 0.8 copy-start.5
  357.5 166.1 %copy-start.1 = (bf16[128,16,128]{0,2,1:T(8,128)(2,1)S(1)}, bf16[128,16,128]{0,2,1:T(8,128)(2,1)}, u32[]{:S(2)}) copy-start(bf16[128,16,128]{0,2,1:T(8,128)(2,1)} %copy.15) | copy-start | bytes 1572868
Sparse Core Ops, SparseCore 0:
  10.1 25.2 all-gather.4
  37.0 22.5 all-gather.2
  67.7 44.4 reduce-scatter.3
  114.5 36.9 reduce-scatter.5
  153.6 25.0 reduce-scatter.7
  357.7 36.7 all-reduce.2
where the time goes:
time: 534 us
  matrix products  362 us (68%)
  waiting for transfers between devices  132 us (25%)
  between operations  14.2 us (3%)
  local copies, waits for them, and re-layouts  12.6 us (2%)
  other arithmetic  7.77 us (1%)
    conv_general_dilated x2, matrix products, depthwise(): lax.conv_general_dilated(source[None], taps[:, None], (1, 1), 'VALID', di...  340 us
    reduce_scatter x1, waiting for transfers between devices, per_device(): lax.psum_scatter(jnp.dot(w_in, preact_grad, preferred_element_type=jnp.fl...  34.7 us
    reduce_scatter x1, waiting for transfers between devices, per_device(): lax.psum_scatter(w_in_local, 'sp', scatter_dimension=1, tiled=True)  28.5 us
    reduce_scatter x1, waiting for transfers between devices, per_device(): lax.psum_scatter(w_out_local, 'sp', scatter_dimension=1, tiled=True)  25.4 us
    all_gather x1, waiting for transfers between devices, per_device(): lax.all_gather(mixed_rows, 'ch', axis=0, tiled=True)  24.1 us
    all_gather x1, waiting for transfers between devices, per_device(): lax.all_gather(grad_rows, 'ch', axis=0, tiled=True)  19.3 us
  transfers between devices with their start and end apart: 8, of which 5 were waited for; matrix products, arithmetic and copies ran while one was open for 36% of the time, Pallas kernels for 0%

commit v1 on v0

--- a/solution.py
+++ b/solution.py
@@ -6,6 +6,22 @@
 
 SQRT_HALF = 0.7071067811865476
 INV_ROOT_TAU = 0.3989422804014327
+
+
+def gather_around(x, axis, dim):
+    ways, here, step = (lax.axis_size(axis), lax.axis_index(axis), x.shape[dim])
+    dims = [n * ways if d == dim else n for d, n in enumerate(x.shape)]
+    full = lax.dynamic_update_slice_in_dim(jnp.zeros(dims, x.dtype), x, here * step, axis=dim)
+    going_up = going_down = x
+    for far in range(1, ways // 2 + 1):
+        going_up = lax.ppermute(going_up, axis, [(d, (d + 1) % ways) for d in range(ways)])
+        full = lax.dynamic_update_slice_in_dim(full, going_up, (here - far) % ways * step, axis=dim)
+        if 2 * far < ways:
+            going_down = lax.ppermute(going_down, axis, [(d, (d - 1) % ways) for d in range(ways)])
+            full = lax.dynamic_update_slice_in_dim(
+                full, going_down, (here + far) % ways * step, axis=dim
+            )
+    return full
 
 
 def with_halo(block, sides, width):
@@ -63,7 +79,7 @@
     mixed_rows = saved_mix.reshape(local_ch, local_pos)
     grad_rows = out_grad.reshape(local_ch, local_pos)
     mixed_all, grad_all = (
-        lax.all_gather(mixed_rows, "ch", axis=0, tiled=True),
+        gather_around(mixed_rows, "ch", 0),
         lax.all_gather(grad_rows, "ch", axis=0, tiled=True),
     )
     hidden, preact_grad = pointwise_back(mixed_all, grad_all, w_in, w_out)

time: 534 us -> 656 us (1.23)
  matrix products: 362 us -> 492 us
  waiting for transfers between devices: 132 us -> 111 us
  starting transfers between devices: 5.13 us -> 14.7 us
    conv_general_dilated x2, matrix products: 340 us -> 471 us  [depthwise(): lax.conv_general_dilated(source[None], taps[:, None], (1, 1), 'VALID', di...]
    all_gather x1 -> x0, waiting for transfers between devices: 24.1 us -> none  [per_device(): lax.all_gather(mixed_rows, 'ch', axis=0, tiled=True)]
    ppermute x0 -> x3, waiting for transfers between devices: none -> 19.8 us  [the longest x2 19.8 us: gather_around(): lax.ppermute(going_up, axis, [(d, (d + 1) % ways) for d in range(ways)])]
    all_gather x1, waiting for transfers between devices: 19.3 us -> 0.01 us  [per_device(): lax.all_gather(grad_rows, 'ch', axis=0, tiled=True)]
    ppermute x0 -> x3, starting transfers between devices: none -> 9.62 us  [the longest x2 7.67 us: gather_around(): lax.ppermute(going_up, axis, [(d, (d + 1) % ways) for d in range(ways)])]
  transfers between devices with their start and end apart: 8 -> 10, of which waited for: 5 -> 5; matrix products, arithmetic and copies ran while one was open for 36% -> 29% of each run, Pallas kernels for 0% -> 0%
where the time goes in v1:
time: 656 us
  matrix products  492 us (75%)
  waiting for transfers between devices  111 us (17%)
  local copies, waits for them, and re-layouts  16.8 us (3%)
  starting transfers between devices  14.7 us (2%)
  between operations  14 us (2%)
  other arithmetic  7.57 us (1%)
    conv_general_dilated x2, matrix products, depthwise(): lax.conv_general_dilated(source[None], taps[:, None], (1, 1), 'VALID', di...  471 us
    reduce_scatter x1, waiting for transfers between devices, per_device(): lax.psum_scatter(jnp.dot(w_in, preact_grad, preferred_element_type=jnp.fl...  37.4 us
    reduce_scatter x1, waiting for transfers between devices, per_device(): lax.psum_scatter(w_out_local, 'sp', scatter_dimension=1, tiled=True)  28.4 us
    reduce_scatter x1, waiting for transfers between devices, per_device(): lax.psum_scatter(w_in_local, 'sp', scatter_dimension=1, tiled=True)  25.4 us
    ppermute x2, waiting for transfers between devices, gather_around(): lax.ppermute(going_up, axis, [(d, (d + 1) % ways) for d in range(ways)])  19.8 us
  transfers between devices with their start and end apart: 10, of which 5 were waited for; matrix products, arithmetic and copies ran while one was open for 29% of the time, Pallas kernels for 0%

profile of v1, /device:TPU:0, one launch (start us, length us, event | category | flops | bytes accessed | tf_op | source)
XLA Modules:
  0.0 655.9 jit_solution(4315637692534376841)
XLA Ops:
  7.2 0.0 copy-start
  7.2 0.0 all-gather.2.cloned.1.call-start
  7.2 2.0 copy.43
  9.3 0.0 all-gather.2.cloned.1.call-update
  9.3 0.0 reduce-scatter.4.cloned.1.call-start
  9.3 2.0 copy.42
  11.4 0.5 collective-permute-start
  11.8 2.0 collective-permute-start.1
  13.8 11.7 %collective-permute-done = bf16[128,2048]{1,0:T(8,128)(2,1)} collective-permute-done((bf16[128,2048]{1,0:T(8,128)(2,1)}, bf16[128,2048]{1,0:T(8,128)(2,1)}, u32[]{:S(2)}, u32[]{:S(2)}) %collective-permute-start) | collective-permute-done | bytes 524320 | tf_op jit(solution)/shard_map/ppermute | solution.py:17
  25.4 7.2 %collective-permute-start.2 = (bf16[128,2048]{1,0:T(8,128)(2,1)}, bf16[128,2048]{1,0:T(8,128)(2,1)}, u32[]{:S(2)}, u32[]{:S(2)}) collective-permute-start(bf16[128,2048]{1,0:T(8,128)(2,1)} %collective-permute-done), channel_id=1, source_target_pairs={{0,4},{4,8},{8,12},{12,0},{1,5},{5,9},{9,13},{13,1},{2,6},{6,10},{... | collective-permute-start | bytes 1572872 | tf_op jit(solution)/shard_map/ppermute | solution.py:17
  32.6 0.2 broadcast_in_dim.13
  32.9 0.0 copy-done.3
  32.9 0.1 constant_dynamic-update-slice_fusion.3
  33.1 1.1 constant_dynamic-update-slice_fusion.2
  34.2 0.0 collective-permute-done.1
  34.2 1.1 constant_dynamic-update-slice_fusion.1
  35.3 8.1 %collective-permute-done.2 = bf16[128,2048]{1,0:T(8,128)(2,1)} collective-permute-done((bf16[128,2048]{1,0:T(8,128)(2,1)}, bf16[128,2048]{1,0:T(8,128)(2,1)}, u32[]{:S(2)}, u32[]{:S(2)}) %collective-permute-start.2) | collective-permute-done | bytes 524320 | tf_op jit(solution)/shard_map/ppermute | solution.py:17
  43.4 1.1 constant_dynamic-update-slice_fusion
  44.5 0.0 copy-done
  44.5 0.0 copy-start.8
  44.5 3.3 fusion.29
  47.8 0.0 copy-done.8
  47.8 4.6 fusion.5
  52.4 0.0 copy-start.1
  52.4 1.3 copy-done.1
  53.7 3.3 convolution_bitcast_fusion
  57.0 0.0 reduce-scatter.4.cloned.1.call-update
  57.1 0.0 reduce-scatter.8.cloned.1.call-start
  57.1 5.2 fusion.23
  62.3 0.0 reduce-scatter.8.cloned.1.call-update
  62.4 0.0 reduce-scatter.6.cloned.1.call-start
  62.4 3.9 fusion.30
  66.3 0.0 reduce-scatter.6.cloned.1.call-update
  66.3 0.0 copy-start.6
  66.3 0.0 all-reduce.3.cloned.1.call-start
  66.3 37.4 %reduce-scatter.4.cloned.1.call-done = f32[128,2048]{0,1:T(8,128)} async-done(((f32[512,2048]{0,1:T(8,128)}), f32[128,2048]{0,1:T(8,128)}) %reduce-scatter.4.cloned.1.call-update) | async-done | bytes 1048592 | tf_op jit(solution)/shard_map/reduce_scatter | solution.py:88
  103.8 1.3 convert_element_type.16
  105.0 0.0 copy-start.5
  105.1 1.0 fusion.28
  106.1 3.4 collective-permute-start.3
  109.5 1.5 collective-permute-start.4
  111.0 0.0 copy-done.4
  111.0 1.2 copy.17
  112.2 0.0 copy-done.6
  112.2 0.9 rev.6
  113.1 0.0 copy-done.5
  113.1 1.5 copy.22
  114.6 28.4 %reduce-scatter.8.cloned.1.call-done = f32[512,128]{1,0:T(8,128)} async-done(((f32[512,512]{1,0:T(8,128)}), f32[512,128]{1,0:T(8,128)}) %reduce-scatter.8.cloned.1.call-update) | async-done | bytes 262160 | tf_op jit(solution)/shard_map/reduce_scatter | solution.py:96
  143.0 1.0 multiply_bitcast_fusion
  144.0 0.8 copy.25
  144.8 25.4 %reduce-scatter.6.cloned.1.call-done = f32[512,128]{1,0:T(8,128)} async-done(((f32[512,512]{1,0:T(8,128)}), f32[512,128]{1,0:T(8,128)}) %reduce-scatter.6.cloned.1.call-update) | async-done | bytes 262160 | tf_op jit(solution)/shard_map/reduce_scatter | solution.py:95
  170.2 1.7 broadcast_multiply_fusion.1
  171.9 0.0 collective-permute-done.3
  171.9 0.0 collective-permute-done.4
  171.9 1.7 fusion.22
  173.6 307.1 %fusion.11 = f32[1,128,31,31]{1,0,3,2:T(1,128)S(1)} fusion(bf16[128,1,16,128]{0,1,3,2:T(2,128)(2,1)} %copy.22, bf16[1,128,46,158]{1,3,2,0:T(8,128)(2,1)S(1)} %fusion.22), kind=kOutput, calls=%fused_computation.17 | convolution fusion | flops 503840768 | bytes 2876928 | tf_op jit(solution)/shard_map/conv_general_dilated | solution.py:41
  480.7 0.0 copy-start.7
  480.7 0.1 copy.44
  480.8 0.9 rev.7
  481.7 0.0 all-reduce.3.cloned.1.call-update
  481.7 164.2 %fusion.13 = f32[1,128,16,128]{1,0,3,2:T(1,128)S(1)} fusion(bf16[1,128,46,158]{1,3,2,0:T(8,128)(2,1)S(1)} %fusion.22, bf16[128,1,31,31]{0,3,2,1:T(8,128)(2,1)S(1)} %bitcast.64), kind=kOutput, calls=%fused_computation.19 | convolution fusion | flops 503840768 | bytes 3155200 | tf_op jit(solution)/shard_map/conv_general_dilated | solution.py:41
  646.0 0.1 convert_add_fusion
  646.1 1.4 copy.24
  647.5 1.9 broadcast_multiply_fusion
  (7 shorter events, 0.0 us)
Async XLA Ops:
  7.2 37.3 %copy-start = (bf16[512,512]{1,0:T(8,128)(2,1)S(1)}, bf16[512,512]{1,0:T(8,128)(2,1)}, u32[]{:S(2)}) copy-start(bf16[512,512]{1,0:T(8,128)(2,1)} %param.10) | copy-start | bytes 1572868
  7.2 40.6 %all-gather.2.cloned.1.call-start = ((), (), s32[]{:S(2)}) async-start(), calls=%async_computation.3 | async-start | bytes 2621440 | tf_op jit(solution)/shard_map/all_gather | solution.py:83
  9.3 23.6 %copy-start.3 = (bf16[128,16,128]{2,1,0:T(8,128)(2,1)S(1)}, bf16[128,16,128]{2,1,0:T(8,128)(2,1)}, u32[]{:S(2)}) copy-start(bf16[128,16,128]{2,1,0:T(8,128)(2,1)} %param.7) | copy-start | bytes 1572868
  9.3 94.5 %reduce-scatter.4.cloned.1.call-start = ((), (), s32[]{:S(2)}) async-start(), calls=%async_computation.4 | async-start | bytes 5242880 | tf_op jit(solution)/shard_map/reduce_scatter | solution.py:88
  11.4 14.1 %collective-permute-start = (bf16[128,2048]{1,0:T(8,128)(2,1)}, bf16[128,2048]{1,0:T(8,128)(2,1)}, u32[]{:S(2)}, u32[]{:S(2)}) collective-permute-start(bf16[128,2048]{1,0:T(8,128)(2,1)} %bitcast.52), channel_id=1, source_target_pairs={{0,4},{4,8},{8,12},{12,0},{1,5},{5,9},{9,13},{13,1},{2,6},{6,10},{... | collective-permute-start | bytes 1572872 | tf_op jit(solution)/shard_map/ppermute | solution.py:17
  11.8 22.4 %collective-permute-start.1 = (bf16[128,2048]{1,0:T(8,128)(2,1)}, bf16[128,2048]{1,0:T(8,128)(2,1)}, u32[]{:S(2)}, u32[]{:S(2)}) collective-permute-start(bf16[128,2048]{1,0:T(8,128)(2,1)} %bitcast.52), channel_id=1, source_target_pairs={{0,12},{4,0},{8,4},{12,8},{1,13},{5,1},{9,5},{13,9},{2,14},{6,2},{... | collective-permute-start | bytes 1572872 | tf_op jit(solution)/shard_map/ppermute | solution.py:20
  25.4 18.0 %collective-permute-start.2 = (bf16[128,2048]{1,0:T(8,128)(2,1)}, bf16[128,2048]{1,0:T(8,128)(2,1)}, u32[]{:S(2)}, u32[]{:S(2)}) collective-permute-start(bf16[128,2048]{1,0:T(8,128)(2,1)} %collective-permute-done), channel_id=1, source_target_pairs={{0,4},{4,8},{8,12},{12,0},{1,5},{5,9},{9,13},{13,1},{2,6},{6,10},{... | collective-permute-start | bytes 1572872 | tf_op jit(solution)/shard_map/ppermute | solution.py:17
  44.5 3.3 copy-start.8
  52.4 1.3 copy-start.1
  57.1 85.9 %reduce-scatter.8.cloned.1.call-start = ((), (), s32[]{:S(2)}) async-start(), calls=%async_computation.7 | async-start | bytes 1310720 | tf_op jit(solution)/shard_map/reduce_scatter | solution.py:96
  62.4 107.9 %reduce-scatter.6.cloned.1.call-start = ((), (), s32[]{:S(2)}) async-start(), calls=%async_computation.6 | async-start | bytes 1310720 | tf_op jit(solution)/shard_map/reduce_scatter | solution.py:95
  66.3 44.7 %copy-start.4 = (bf16[128,16,128]{2,1,0:T(8,128)(2,1)S(1)}, bf16[128,16,128]{2,1,0:T(8,128)(2,1)}, u32[]{:S(2)}) copy-start(bf16[128,16,128]{2,1,0:T(8,128)(2,1)} %param.8) | copy-start | bytes 1572868
  66.3 45.9 %copy-start.6 = (bf16[128,31,31]{0,2,1:T(8,128)(2,1)S(1)}, bf16[128,31,31]{0,2,1:T(8,128)(2,1)}, u32[]{:S(2)}) copy-start(bf16[128,31,31]{0,2,1:T(8,128)(2,1)} %param.9) | copy-start | bytes 738052
  66.3 581.2 %all-reduce.3.cloned.1.call-start = ((), (), s32[]{:S(2)}) async-start(), calls=%async_computation.5 | async-start | bytes 1015808 | tf_op jit(solution)/shard_map/psum | solution.py:103
  105.0 8.1 %copy-start.5 = (bf16[128,16,128]{2,1,0:T(8,128)(2,1)S(1)}, bf16[128,16,128]{2,1,0:T(8,128)(2,1)}, u32[]{:S(2)}) copy-start(bf16[128,16,128]{2,1,0:T(8,128)(2,1)} %param.6) | copy-start | bytes 1572868
  106.1 65.8 %collective-permute-start.3 = (bf16[128,15,128]{0,2,1:T(8,128)(2,1)}, bf16[128,15,128]{0,2,1:T(8,128)(2,1)S(1)}, u32[]{:S(2)}, u32[]{:S(2)}) collective-permute-start(bf16[128,15,128]{0,2,1:T(8,128)(2,1)} %get-tuple-element.12), channel_id=1, source_target_pairs={{0,1},{1,2},{2,3},{4,5},{5,6},{6,7},{8,9},{9,10},{10,11},{12,13},{... | collective-permute-start | bytes 1474568 | tf_op jit(solution)/shard_map/ppermute | solution.py:32
  109.5 62.4 %collective-permute-start.4 = (bf16[128,15,128]{0,2,1:T(8,128)(2,1)S(1)}, bf16[128,15,128]{0,2,1:T(8,128)(2,1)}, u32[]{:S(2)}, u32[]{:S(2)}) collective-permute-start(bf16[128,15,128]{0,2,1:T(8,128)(2,1)S(1)} %get-tuple-element.13), channel_id=1, source_target_pairs={{1,0},{2,1},{3,2},{5,4},{6,5},{7,6},{9,8},{10,9},{11,10},{13,12},{... | collective-permute-start | bytes 1474568 | tf_op jit(solution)/shard_map/ppermute | solution.py:35
  480.7 1.0 copy-start.7
  481.7 164.2 %copy-start.2 = (bf16[128,16,128]{0,2,1:T(8,128)(2,1)S(1)}, bf16[128,16,128]{0,2,1:T(8,128)(2,1)}, u32[]{:S(2)}) copy-start(bf16[128,16,128]{0,2,1:T(8,128)(2,1)} %copy.17) | copy-start | bytes 1572868
Sparse Core Ops, SparseCore 0:
  9.6 33.3 all-gather.1
  57.2 46.5 reduce-scatter.3
  106.2 36.7 reduce-scatter.7
  145.1 25.0 reduce-scatter.5
  481.8 36.7 all-reduce.2
